TPU v7x, 32 devices: a whole 2x2x4 slice. The times are simulated.
32 devices in a mesh: layers: 2 (over y), rows: 4 (over z), cols: 4 (over x, core).
Axes of the slice: x: 2, y: 2, z: 4, core: 2. Of those that a mesh axis runs over, the one named last changes fastest.
Arguments:
- weight: bfloat16 [2048, 16384], P(('layers', 'rows'), 'cols'), parts along dimension 0, may hold values from -6 to 6
- update: bfloat16 [2048, 16384], P(('layers', 'rows'), 'cols'), parts along dimension 0, may hold values from -4 to 4
- keep_codes: int32 [2048, 2048], P(('layers', 'rows'), 'cols'), parts along dimension 0, may hold values from 0 to 35
- chol_factor: bfloat16 [32768, 16384], P(('layers', 'cols'), 'rows'), parts along dimension 0, as said below
- sketch: bfloat16 [16384, 256], P('rows'), may hold values from -6 to 6
Outputs:
- adapter_a: bfloat16 [2048, 256], P(('layers', 'rows')), parts along dimension 0
- adapter_b: bfloat16 [512, 16384], P(('layers', 'rows'), 'cols'), parts along dimension 0
There are 2 independent parts, one for each index of `layers`. A program takes and returns all parts, laid end to end along the dimension named above; an argument that names none is the same for every part. Nothing has to cross between parts.
Inputs may be any that keep to these rules, and one draw needn't show every extreme that they name: `keep_codes`: each code is a pair of 2:4 patterns, the first in code % 6 and the second in code // 6. chol_factor is lower triangular with a positive diagonal.
All inputs are finite; a program needn't handle non-finite values.
Results may differ from a plain program's by a relative error of at most 0.006.
Values may be sent and summed in bfloat16 or wider, within the bound.
A program may use at most 128 MiB of HBM per device.

v0:
```python
import math

import jax
import jax.numpy as jnp
from jax import lax
from jax.sharding import PartitionSpec as P


def decode_keep(codes):
    first = codes % 6
    second = codes // 6
    columns = []
    for part_code in (first, second):
        columns.append(((part_code == 0) | (part_code == 1) | (part_code == 2)).astype(jnp.float32))
        columns.append(((part_code == 0) | (part_code == 3) | (part_code == 4)).astype(jnp.float32))
        columns.append(((part_code == 1) | (part_code == 3) | (part_code == 5)).astype(jnp.float32))
        columns.append(((part_code == 2) | (part_code == 4) | (part_code == 5)).astype(jnp.float32))
    stacked = jnp.stack(columns, axis=-1)
    return stacked.reshape(codes.shape[0], codes.shape[1] * 8)


def gram_of(sample):
    return jnp.dot(
        sample.T, sample, precision=lax.Precision.HIGHEST, preferred_element_type=jnp.float32
    )


def finish(sample, gram_matrix, root_rows):
    lower_factor = jnp.linalg.cholesky(gram_matrix)
    basis_cols = lax.linalg.triangular_solve(
        lower_factor, sample, left_side=False, lower=True, transpose_a=True
    )
    return (root_rows * basis_cols).astype(jnp.bfloat16)


def shards(weight, update, keep_codes, chol_factor, sketch):
    root_rows = math.sqrt(weight.shape[0] * lax.axis_size("rows"))
    kept_mask = decode_keep(keep_codes)
    weight_f = weight.astype(jnp.float32)
    prune_error = (weight_f - kept_mask * (weight_f + update.astype(jnp.float32))).astype(
        jnp.bfloat16
    )
    own_share = lax.psum_scatter(
        jnp.dot(chol_factor, sketch, preferred_element_type=jnp.float32),
        "rows",
        scatter_dimension=0,
        tiled=True,
    ).astype(jnp.bfloat16)
    whitened = lax.all_gather(own_share, "rows", axis=0, tiled=True)
    partial_sample = jnp.dot(prune_error, whitened, preferred_element_type=jnp.float32)
    sample = lax.psum(partial_sample, "cols")
    gram_matrix = lax.psum(gram_of(sample), "rows")
    adapter_a = finish(sample, gram_matrix, root_rows)
    adapter_b = (
        lax.psum_scatter(
            lax.dot_general(
                adapter_a, prune_error, (((0,), (0,)), ((), ())), preferred_element_type=jnp.float32
            ),
            "rows",
            scatter_dimension=0,
            tiled=True,
        )
        / root_rows
    ).astype(jnp.bfloat16)
    return (adapter_a, adapter_b)


def solution(mesh):
    in_specs = (
        P(("layers", "rows"), "cols"),
        P(("layers", "rows"), "cols"),
        P(("layers", "rows"), "cols"),
        P(("layers", "cols"), "rows"),
        P("rows", None),
    )
    out_specs = (P(("layers", "rows"), None), P(("layers", "rows"), "cols"))
    return jax.shard_map(shards, mesh=mesh, in_specs=in_specs, out_specs=out_specs, check_vma=False)
```

profile of v0, /device:TPU:0, one launch (start us, length us, event | category | flops | bytes accessed | tf_op | source)
XLA Modules:
  0.0 392.8 jit_solution(16210084310277697815)
XLA Ops:
  7.2 0.0 copy-start
  7.2 0.0 reduce-scatter.3.cloned.1.call-start
  7.2 1.5 copy-done
  8.8 17.0 %fusion.17 = f32[4096,256]{1,0:T(8,128)} fusion(bf16[4096,4096]{1,0:T(8,128)(2,1)} %param.8, bf16[4096,256]{1,0:T(8,128)(2,1)S(1)} %copy-done), kind=kOutput, calls=%fused_computation.62 | convolution fusion | flops 8589934592 | bytes 39845888 | tf_op jit(solution)/shard_map/dot_general | solution.py:44
  25.8 0.0 reduce-scatter.3.cloned.1.call-update
  25.8 0.0 all-gather.2.cloned.1.call-start
  25.9 79.6 %reduce-scatter.3.cloned.1.call-done = f32[1024,256]{1,0:T(8,128)} async-done(((f32[4096,256]{1,0:T(8,128)}), f32[1024,256]{1,0:T(8,128)}) %reduce-scatter.3.cloned.1.call-update) | async-done | bytes 1048592 | tf_op jit(solution)/shard_map/reduce_scatter | solution.py:43
  105.4 2.1 convert_element_type.29
  107.5 0.0 all-gather.2.cloned.1.call-update
  107.5 0.0 all-reduce.4.cloned.1.call-start
  107.6 4.1 %copy.25 = bf16[256,4096]{0,1:T(8,128)(2,1)} copy(bf16[256,4096]{1,0:T(8,128)(2,1)} %param.5) | data formatting | bytes 4194304 | tf_op args[0]
  111.6 0.0 copy-start.1
  111.6 4.2 %copy.27 = bf16[256,4096]{0,1:T(8,128)(2,1)} copy(bf16[256,4096]{1,0:T(8,128)(2,1)} %param.6) | data formatting | bytes 4194304 | tf_op args[1]
  115.8 0.0 copy-done.1
  115.8 1.2 bitcast_dynamic-update-slice_fusion.8
  117.0 1.1 bitcast_dynamic-update-slice_fusion.7
  118.1 1.1 bitcast_dynamic-update-slice_fusion.6
  119.2 0.8 bitcast_dynamic-update-slice_fusion.5
  120.0 1.3 bitcast_dynamic-update-slice_fusion.4
  121.2 0.9 bitcast_dynamic-update-slice_fusion.3
  122.1 0.8 bitcast_dynamic-update-slice_fusion.2
  122.9 0.8 bitcast_dynamic-update-slice_fusion.1
  123.7 3.4 copy.26
  127.1 27.0 %all-gather.2.cloned.1.call-done = bf16[4096,256]{1,0:T(8,128)(2,1)} async-done(((bf16[1024,256]{1,0:T(8,128)(2,1)}), bf16[4096,256]{1,0:T(8,128)(2,1)}) %all-gather.2.cloned.1.call-update) | async-done | bytes 2097168 | tf_op jit(solution)/shard_map/all_gather | solution.py:49
  154.1 4.8 %fusion.14 = f32[256,256]{1,0:T(8,128)} fusion(bf16[4096,256]{1,0:T(8,128)(2,1)} %all-gather.2.cloned.1.call-done, bf16[256,4096]{0,1:T(8,128)(2,1)} %copy.25, bf16[256,4096]{0,1:T(8,128)(2,1)} %copy.27, pred[256,512,8]{0,2,1:T(8,128)(4,1)S(1)} %copy.26), kind=kOutput, calls=%fused_computation.60 | convolution fusion | flops 543162368 | bytes 7602176 | tf_op jit(solution)/shard_map/dot_general | solution.py:50
  158.9 0.0 all-reduce.4.cloned.1.call-update
  158.9 0.0 all-reduce.6.cloned.1.call-start
  159.0 30.8 %all-reduce.4.cloned.1.call-done = f32[256,256]{1,0:T(8,128)} async-done(((f32[256,256]{1,0:T(8,128)}), f32[256,256]{1,0:T(8,128)}) %all-reduce.4.cloned.1.call-update) | async-done | bytes 262160 | tf_op jit(solution)/shard_map/psum | solution.py:51
  189.7 2.3 fusion.18
  192.1 0.0 copy-start.2
  192.1 0.0 all-reduce.6.cloned.1.call-update
  192.1 0.2 reduce-scatter.5.cloned.1.call-start
  192.3 35.5 %all-reduce.6.cloned.1.call-done = f32[256,256]{0,1:T(8,128)} async-done(((f32[256,256]{0,1:T(8,128)}), f32[256,256]{0,1:T(8,128)}) %all-reduce.6.cloned.1.call-update) | async-done | bytes 262160 | tf_op jit(solution)/shard_map/psum | solution.py:52
  227.9 1.8 copy.29
  229.6 1.1 fusion.4
  230.7 0.0 copy-start.3
  230.7 0.7 copy-done.3
  231.4 11.7 %cholesky.50 = f32[128,128]{1,0:T(8,128)S(1)} custom-call(f32[128,128]{1,0:T(8,128)S(1)} %cholesky.118), custom_call_target="Cholesky" | custom-call | tf_op jit(solution)/shard_map/jit(cholesky)/cholesky | solution.py:29
  243.2 0.7 cholesky.113
  243.9 9.8 %custom-call.14 = f32[1,128,128]{1,2,0:T(8,128)S(1)} custom-call(f32[1,128,128]{2,1,0:T(8,128)S(1)} %get-tuple-element.48), custom_call_target="InvertDiagBlocksLowerTriangular" | custom-call | tf_op jit(solution)/shard_map/jit(cholesky)/cholesky | solution.py:29
  253.7 1.7 constant_dynamic-update-slice_fusion.1
  255.4 1.1 convolution_subtract_fusion.1
  256.5 11.7 %cholesky.105 = f32[128,128]{1,0:T(8,128)S(1)} custom-call(f32[128,128]{1,0:T(8,128)S(1)} %convolution_subtract_fusion.1), custom_call_target="Cholesky" | custom-call | tf_op jit(solution)/shard_map/jit(cholesky)/cholesky | solution.py:29
  268.2 0.6 select_reduce_fusion
  268.8 0.7 compare_reduce_fusion
  270.8 1.7 select_select_fusion
  272.5 0.1 triangular_solve.58
  272.5 7.0 %while.1 = (s32[]{:T(128)}, f32[256,256]{1,0:T(8,128)}, s32[2,2]{1,0:T(2,128)S(1)}, f32[2,128,128]{2,1,0:T(8,128)}, s32[]{:T(128)}) while((s32[]{:T(128)}, f32[256,256]{1,0:T(8,128)}, s32[2,2]{1,0:T(2,128)S(1)}, f32[2,128,128]{2,1,0:T(8,128)}, s32[]{:T(128)}) %tuple.43), condition=%wide.while_cond, body=%wide.while_body.sunk | while | flops 2 | bytes 132205 | solution.py:30
  272.6 0.6 fusion.30
  273.2 2.9 bitcast_dynamic-update-slice_fusion.10
  276.1 0.6 fusion.30
  276.7 2.8 bitcast_dynamic-update-slice_fusion.10
  279.5 20.5 %custom-call.15 = f32[2,128,128]{1,2,0:T(8,128)S(1)} custom-call(f32[2,128,128]{2,1,0:T(8,128)} %get-tuple-element.9), custom_call_target="InvertDiagBlocksLowerTriangular" | custom-call | tf_op jit(solution)/shard_map/triangular_solve | solution.py:30
  300.0 0.0 copy-done.2
  300.0 0.3 fusion.5
  300.4 1.2 convolution_subtract_fusion
  301.6 0.3 fusion.7
  302.0 5.5 %fusion.12 = f32[256,4096]{1,0:T(8,128)} fusion(bf16[256,256]{0,1:T(8,128)(2,1)S(1)} %fusion.3, bf16[256,4096]{0,1:T(8,128)(2,1)} %copy.25, bf16[256,4096]{0,1:T(8,128)(2,1)} %copy.27, pred[256,512,8]{0,2,1:T(8,128)(4,1)S(1)} %copy.26), kind=kOutput, calls=%fused_computation.59 | convolution fusion | flops 543162368 | bytes 9568256 | tf_op jit(solution)/shard_map/dot_general | solution.py:56
  307.5 0.0 reduce-scatter.5.cloned.1.call-update
  307.5 0.8 copy.30
  308.3 75.9 %reduce-scatter.5.cloned.1.call-done = f32[64,4096]{1,0:T(8,128)} async-done(((f32[256,4096]{1,0:T(8,128)}), f32[64,4096]{1,0:T(8,128)}) %reduce-scatter.5.cloned.1.call-update) | async-done | bytes 1048592 | tf_op jit(solution)/shard_map/reduce_scatter | solution.py:55
  384.2 2.1 multiply_convert_fusion
  (7 shorter events, 0.1 us)
Async XLA Ops:
  7.2 1.6 copy-start
  7.2 98.2 %reduce-scatter.3.cloned.1.call-start = ((), (), s32[]{:S(2)}) async-start(), calls=%async_computation.2 | async-start | bytes 5242880 | tf_op jit(solution)/shard_map/reduce_scatter | solution.py:43
  25.8 128.3 %all-gather.2.cloned.1.call-start = ((), (), s32[]{:S(2)}) async-start(), calls=%async_computation.3 | async-start | bytes 2621440 | tf_op jit(solution)/shard_map/all_gather | solution.py:49
  107.5 82.2 %all-reduce.4.cloned.1.call-start = ((), (), s32[]{:S(2)}) async-start(), calls=%async_computation.4 | async-start | bytes 524288 | tf_op jit(solution)/shard_map/psum | solution.py:51
  111.6 4.2 %copy-start.1 = (s32[256,512]{1,0:T(8,128)S(1)}, s32[256,512]{1,0:T(8,128)}, u32[]{:S(2)}) copy-start(s32[256,512]{1,0:T(8,128)} %param.7) | copy-start | bytes 1572868
  158.9 68.9 %all-reduce.6.cloned.1.call-start = ((), (), s32[]{:S(2)}) async-start(), calls=%async_computation.5 | async-start | bytes 524288 | tf_op jit(solution)/shard_map/psum | solution.py:52
  192.1 108.0 %copy-start.2 = (f32[256,256]{1,0:T(8,128)S(1)}, f32[256,256]{1,0:T(8,128)}, u32[]{:S(2)}) copy-start(f32[256,256]{1,0:T(8,128)} %all-reduce.4.cloned.1.call-done) | copy-start | bytes 786436
  192.1 192.1 %reduce-scatter.5.cloned.1.call-start = ((), (), s32[]{:S(2)}) async-start(), calls=%async_computation.6 | async-start | bytes 5242880 | tf_op jit(solution)/shard_map/reduce_scatter | solution.py:55
  230.7 0.7 copy-start.3
Sparse Core Ops, SparseCore 0:
  25.9 79.4 reduce-scatter.2
  107.6 46.4 all-gather.1
  159.0 30.6 all-reduce.3
  192.5 35.3 all-reduce.5
  307.6 76.4 reduce-scatter.4
where the time goes:
time: 394 us; the launch traced here: 393 us
  waiting for transfers between devices  249 us (63%)
  other arithmetic  69.9 us (18%)
  matrix products  34.3 us (9%)
  local copies, waits for them, and re-layouts  24.2 us (6%)
  between operations  15.1 us (4%)
    reduce_scatter x1, waiting for transfers between devices, shards(): lax.psum_scatter(jnp.dot(chol_factor, sketch, preferred_element_type=jnp....  79.6 us
    reduce_scatter x1, waiting for transfers between devices, shards(): lax.psum_scatter(lax.dot_general(adapter_a, prune_error, (((0,), (0,)), (...  75.9 us
    psum x1, waiting for transfers between devices, shards(): gram_matrix = lax.psum(gram_of(sample), 'rows')  35.5 us
    another operation x6, other arithmetic, finish(): lower_factor = jnp.linalg.cholesky(gram_matrix)  34.6 us
    psum x1, waiting for transfers between devices, shards(): sample = lax.psum(partial_sample, 'cols')  30.8 us
    all_gather x1, waiting for transfers between devices, shards(): whitened = lax.all_gather(own_share, 'rows', axis=0, tiled=True)  27 us
    another operation x3, other arithmetic, finish(): lax.linalg.triangular_solve(lower_factor, sample, left_side=False, lower=...  22.2 us
    dot_general x1, matrix products, shards(): jnp.dot(chol_factor, sketch, preferred_element_type=jnp.float32)  17 us
  transfers between devices with their start and end apart: 5, of which 5 were waited for; matrix products, arithmetic and copies ran while one was open for 5% of the time, Pallas kernels for 0%

commit v1 on v0

v1 whole, which is shorter than its diff:
```python
import functools
import math

import jax
import jax.numpy as jnp
from jax import lax
from jax.experimental import pallas as pl
from jax.experimental.pallas import tpu as pltpu
from jax.sharding import PartitionSpec as P

MESH = pl.DeviceIdType.MESH
F32 = jnp.float32
BF16 = jnp.bfloat16
NCHUNK = 8
WORDS = 128

HI = lax.Precision.HIGHEST

def chol_steps(m_ref, w_ref, n, nseg):
    row = lax.broadcasted_iota(jnp.int32, (n, n), 0)
    col = lax.broadcasted_iota(jnp.int32, (n, n), 1)
    w_ref[...] = jnp.where(row == col, 1.0, 0.0).astype(jnp.float32)
    seg = n // nseg
    sub = lax.broadcasted_iota(jnp.int32, (8, 128), 0)
    for s in range(nseg):
        base = s * seg
        rows = n - base
        width = max(128, -(-rows // 128) * 128)
        wwidth = max(128, -(-(base + seg) // 128) * 128)
        rid = lax.broadcasted_iota(jnp.int32, (rows, 128), 0) + base

        def body(i, carry, base=base, rows=rows, width=width, wwidth=wwidth, rid=rid):
            r0 = pl.multiple_of(base + i * 8, 8)
            m = m_ref[base:n, :width]
            c = [jnp.broadcast_to(m[:, j:j + 1], (rows, 128)) for j in range(8)]
            b8 = m_ref[pl.ds(r0, 8), 0:128]
            p = [jnp.broadcast_to(b8[:, j:j + 1], (8, 128)) for j in range(8)]
            rm = m_ref[pl.ds(r0, 8), :width]
            rw = w_ref[pl.ds(r0, 8), :wwidth]
            below = rid >= r0 + 8
            mrows, wrows, cs = [], [], []
            for j in range(8):
                rs = lax.rsqrt(p[j][j:j + 1, :])
                pj = p[j] * rs
                cj = c[j] * rs
                mj = rm[j:j + 1] * jnp.tile(rs, (1, width // 128))
                wj = rw[j:j + 1] * jnp.tile(rs, (1, wwidth // 128))
                for k in range(j + 1, 8):
                    sc = pj[k:k + 1, :]
                    p[k] = p[k] - pj * sc
                    c[k] = c[k] - cj * sc
                pm = jnp.where(sub > j, pj, 0.0)
                rm = rm - jnp.tile(pm, (1, width // 128)) * mj
                rw = rw - jnp.tile(pm, (1, wwidth // 128)) * wj
                mrows.append(mj)
                wrows.append(wj)
                cs.append(jnp.where(below, cj, 0.0))
            w = w_ref[base:n, :wwidth]
            for j in range(8):
                m = m - jnp.tile(cs[j], (1, width // 128)) * mrows[j]
                w = w - jnp.tile(cs[j], (1, wwidth // 128)) * wrows[j]
            w_ref[base:n, :wwidth] = w
            w_ref[pl.ds(r0, 8), :wwidth] = jnp.concatenate(wrows, axis=0)
            m_ref[base:n, :width] = pltpu.roll(m, width - 8, 1)
            return carry

        lax.fori_loop(0, seg // 8, body, 0)

def finish_kernel(root, g_ref, s_ref, a_ref, m_ref, w_ref):
    n = g_ref.shape[0]
    m_ref[...] = g_ref[...]
    chol_steps(m_ref, w_ref, n, 4)
    basis = lax.dot_general(s_ref[...], w_ref[...], (((1,), (1,)), ((), ())), precision=HI, preferred_element_type=jnp.float32)
    a_ref[...] = (root * basis).astype(jnp.bfloat16)

def finish(gram, sample, root):
    n = gram.shape[0]
    return pl.pallas_call(functools.partial(finish_kernel, root),
        out_shape=jax.ShapeDtypeStruct(sample.shape, jnp.bfloat16),
        in_specs=[pl.BlockSpec(memory_space=pltpu.VMEM)] * 2,
        out_specs=pl.BlockSpec(memory_space=pltpu.VMEM),
        scratch_shapes=[pltpu.VMEM((n, n), jnp.float32)] * 2,
        compiler_params=pltpu.CompilerParams(vmem_limit_bytes=32 << 20))(gram, sample)


def copy_to(src, dst, send, recv, axis, index):
    return pltpu.make_async_remote_copy(
        src_ref=src, dst_ref=dst, send_sem=send, recv_sem=recv, device_id={axis: index}, device_id_type=MESH
    )


def greet(axes):
    barrier = pltpu.get_barrier_semaphore()
    count = 0
    for axis, size in axes:
        me = lax.axis_index(axis)
        for d in range(1, size):
            pl.semaphore_signal(barrier, inc=1, device_id={axis: lax.rem(me + d, size)}, device_id_type=MESH)
            count += 1
    pl.semaphore_wait(barrier, count)


def sample_kernel(
    n, nc, w_hbm, u_hbm, k_hbm, l_hbm, s_hbm, pe_ref, sample_ref, gram_ref,
    w_v, u_v, k_v, s_v, l_v, expand, own, recv_p, recv_s, send_p, send_s, acc, rs_recv, samp, gpart, gz, gfull,
    in_sem, l_sem, sp_sem, rp_sem, ss_sem, rsv_sem, a_send, a_recv, b_send, b_recv, c_send, c_recv, d_send, d_recv,
):
    r = lax.axis_index("rows")
    c = lax.axis_index("cols")
    rank = s_v.shape[1]
    block, depth = l_hbm.shape
    ck = block // NCHUNK
    local_rows, width = w_v.shape
    pe_steps = width // (8 * WORDS)
    nonzero = (c + 1) * block > r * depth
    has_p = r > 0
    has_s = jnp.logical_and(r < n - 1, (c + 1) * block > (r + 1) * depth)
    give_s = jnp.logical_and(r > 0, nonzero)
    rr = n - 1 - r

    def load(t):
        return pltpu.make_async_copy(l_hbm.at[pl.ds(pl.multiple_of(t * ck, ck), ck), :], l_v.at[lax.rem(t, 2)], l_sem.at[lax.rem(t, 2)])

    ins = [pltpu.make_async_copy(a, b, in_sem.at[i]) for i, (a, b) in enumerate(((s_hbm, s_v), (w_hbm, w_v), (u_hbm, u_v), (k_hbm, k_v)))]
    ins[0].start()

    @pl.when(nonzero)
    def _():
        load(0).start()

    for one in ins[1:]:
        one.start()
    word = lax.broadcasted_iota(jnp.int32, (WORDS, 8 * WORDS), 0)
    lane = lax.broadcasted_iota(jnp.int32, (WORDS, 8 * WORDS), 1)
    expand[...] = jnp.where(lax.shift_right_logical(lane, 3) == word, 1.0, 0.0).astype(BF16)
    acc[...] = jnp.zeros_like(acc)
    greet((("rows", n), ("cols", nc)))
    for one in ins:
        one.wait()

    def forward(j):
        return copy_to(send_p.at[j], recv_p.at[j], sp_sem.at[j], rp_sem.at[j], "rows", lax.rem(r + 1, n))

    def backward(j):
        return copy_to(send_s.at[j], recv_s.at[j], ss_sem.at[j], rsv_sem.at[j], "rows", lax.rem(r + n - 1, n))

    def step(t, carry):
        @pl.when(jnp.logical_and(t < NCHUNK, nonzero))
        def _():
            @pl.when(t + 1 < NCHUNK)
            def _():
                load(t + 1).start()

            load(t).wait()
            own[t] = jnp.dot(l_v[lax.rem(t, 2)], s_v[...], preferred_element_type=F32)

        @pl.when(jnp.logical_and(t < NCHUNK, jnp.logical_not(nonzero)))
        def _():
            own[t] = jnp.zeros((ck, rank), F32)

        p = t - r

        @pl.when(jnp.logical_and(p >= 0, p < NCHUNK))
        def _():
            @pl.when(has_p)
            def _():
                forward(p).wait_recv()

            @pl.when(r < n - 1)
            def _():
                @pl.when(has_p)
                def _():
                    send_p[p] = (own[p] + recv_p[p].astype(F32)).astype(BF16)

                @pl.when(jnp.logical_not(has_p))
                def _():
                    send_p[p] = own[p].astype(BF16)

                forward(p).start()

        s = t - rr

        @pl.when(jnp.logical_and(s >= 0, s < NCHUNK))
        def _():
            @pl.when(has_s)
            def _():
                backward(s).wait_recv()

            @pl.when(give_s)
            def _():
                @pl.when(has_s)
                def _():
                    send_s[s] = (own[s] + recv_s[s].astype(F32)).astype(BF16)

                @pl.when(jnp.logical_not(has_s))
                def _():
                    send_s[s] = own[s].astype(BF16)

                backward(s).start()

        @pl.when(t < pe_steps)
        def _():
            codes = k_v[:, pl.ds(pl.multiple_of(t * WORDS, WORDS), WORDS)]
            second = lax.shift_right_logical(codes * 43, 8)
            first = codes - 6 * second
            table = jnp.full(codes.shape, 0xCA6953, jnp.int32)
            low = lax.shift_right_logical(table, 4 * first) & 15
            high = lax.shift_right_logical(table, 4 * second) & 15
            packed = (low + 16 * high).astype(F32).astype(BF16)
            spread = jnp.dot(packed, expand[...], preferred_element_type=F32).astype(jnp.int32)
            bit = jnp.left_shift(1, lax.broadcasted_iota(jnp.int32, spread.shape, 1) & 7)
            at = pl.ds(pl.multiple_of(t * 8 * WORDS, 8 * WORDS), 8 * WORDS)
            wv = w_v[:, at].astype(F32)
            uv = u_v[:, at].astype(F32)
            pe_ref[:, at] = (wv - jnp.where((spread & bit) != 0, wv + uv, 0.0)).astype(BF16)

        m = t - jnp.maximum(r, rr)

        @pl.when(jnp.logical_and(m >= 0, m < NCHUNK))
        def _():
            @pl.when(has_p)
            def _():
                own[m] = own[m] + recv_p[m].astype(F32)

            @pl.when(has_s)
            def _():
                own[m] = own[m] + recv_s[m].astype(F32)

            part = jnp.dot(pe_ref[:, pl.ds(pl.multiple_of(m * ck, ck), ck)], own[m].astype(BF16), preferred_element_type=F32)
            acc[...] += part.reshape(acc.shape)

        return carry

    lax.fori_loop(0, NCHUNK + n - 1, step, 0)

    def drain(j, carry):
        @pl.when(r < n - 1)
        def _():
            forward(j).wait_send()

        @pl.when(give_s)
        def _():
            backward(j).wait_send()

        return carry

    def peers(size, me):
        return [lax.rem(me + d, size) for d in range(1, size)]

    def swap(copies_out, copies_in):
        for one in copies_out:
            one.start()
        for one in copies_in:
            one.wait_recv()

    def exchange(src_of, dst, send, recv, axis, size, me):
        out = [copy_to(src_of(p), dst.at[me], send.at[p], recv.at[me], axis, p) for p in peers(size, me)]
        back = [copy_to(src_of(p), dst.at[p], send.at[p], recv.at[p], axis, p) for p in peers(size, me)]
        swap(out, back)
        return out

    sent = exchange(lambda p: acc.at[p], rs_recv, a_send, a_recv, "cols", nc, c)
    total = acc[c]
    for p in peers(nc, c):
        total = total + rs_recv[p]
    samp[c] = total
    sent += exchange(lambda p: samp.at[c], samp, b_send, b_recv, "cols", nc, c)
    sample = samp[...].reshape(local_rows, rank)
    sample_ref[...] = sample
    gpart[...] = lax.dot_general(
        sample, sample, (((0,), (0,)), ((), ())), precision=HI, preferred_element_type=F32
    ).reshape(gpart.shape)
    sent += exchange(lambda p: gpart.at[c], gz, c_send, c_recv, "rows", n, r)
    total = gpart[c]
    for p in peers(n, r):
        total = total + gz[p]
    gfull[c] = total
    sent += exchange(lambda p: gfull.at[c], gfull, d_send, d_recv, "cols", nc, c)
    gram_ref[...] = gfull[...].reshape(rank, rank)
    lax.fori_loop(0, NCHUNK, drain, 0)
    for one in sent:
        one.wait_send()


def sample_and_gram(n, nc, weight, update, codes, factor, sketch):
    rows, width = weight.shape
    block, depth = factor.shape
    rank = sketch.shape[1]
    ck = block // NCHUNK
    chunks = (NCHUNK, ck, rank)
    vm = pl.BlockSpec(memory_space=pltpu.VMEM)
    dma = pltpu.SemaphoreType.DMA
    return pl.pallas_call(
        functools.partial(sample_kernel, n, nc),
        out_shape=(
            jax.ShapeDtypeStruct((rows, width), BF16),
            jax.ShapeDtypeStruct((rows, rank), F32),
            jax.ShapeDtypeStruct((rank, rank), F32),
        ),
        in_specs=[pl.BlockSpec(memory_space=pl.ANY)] * 5,
        out_specs=(vm, vm, vm),
        scratch_shapes=[
            pltpu.VMEM((rows, width), BF16),
            pltpu.VMEM((rows, width), BF16),
            pltpu.VMEM(codes.shape, jnp.int32),
            pltpu.VMEM(sketch.shape, BF16),
            pltpu.VMEM((2, ck, depth), BF16),
            pltpu.VMEM((WORDS, 8 * WORDS), BF16),
            pltpu.VMEM(chunks, F32),
            pltpu.VMEM(chunks, BF16),
            pltpu.VMEM(chunks, BF16),
            pltpu.VMEM(chunks, BF16),
            pltpu.VMEM(chunks, BF16),
            pltpu.VMEM((nc, rows // nc, rank), F32),
            pltpu.VMEM((nc, rows // nc, rank), F32),
            pltpu.VMEM((nc, rows // nc, rank), F32),
            pltpu.VMEM((nc, rank // nc, rank), F32),
            pltpu.VMEM((n, rank // nc, rank), F32),
            pltpu.VMEM((nc, rank // nc, rank), F32),
            dma((4,)),
            dma((2,)),
            dma((NCHUNK,)),
            dma((NCHUNK,)),
            dma((NCHUNK,)),
            dma((NCHUNK,)),
            dma((nc,)),
            dma((nc,)),
            dma((nc,)),
            dma((nc,)),
            dma((n,)),
            dma((n,)),
            dma((nc,)),
            dma((nc,)),
        ],
        compiler_params=pltpu.CompilerParams(collective_id=0, has_side_effects=True, vmem_limit_bytes=52 << 20),
        name="sample_and_gram",
    )(weight, update, codes, factor, sketch)


def second_kernel(n, q_count, root, a_ref, pe_ref, out_ref, own, recv_p, recv_s, send_p, send_s, sp_sem, rp_sem, ss_sem, rs_sem):
    r = lax.axis_index("rows")
    rr = n - 1 - r
    share, width = out_ref.shape
    cq = width // q_count
    items = (n - 1) * q_count
    a_t = a_ref[...]

    def fill(q, carry):
        at = pl.ds(pl.multiple_of(q * cq, cq), cq)
        part = lax.dot_general(a_t, pe_ref[:, at], (((0,), (0,)), ((), ())), preferred_element_type=F32)
        own[:, :, at] = part.reshape(n, share, cq)
        return carry

    lax.fori_loop(0, q_count, fill, 0)
    greet((("rows", n),))

    def forward(e):
        return copy_to(send_p.at[e], recv_p.at[e], sp_sem.at[e], rp_sem.at[e], "rows", lax.rem(r + 1, n))

    def backward(e):
        return copy_to(send_s.at[e], recv_s.at[e], ss_sem.at[e], rs_sem.at[e], "rows", lax.rem(r + n - 1, n))

    def pass_on(e, place, target, t, copy, recv, send):
        at = pl.ds(pl.multiple_of((e % q_count) * cq, cq), cq)

        @pl.when(jnp.logical_and(place > 0, place <= target))
        def _():
            copy(e).wait_recv()
            own[t, :, at] = own[t, :, at] + recv[e].astype(F32)

        @pl.when(place < target)
        def _():
            send[e] = own[t, :, at].astype(BF16)
            copy(e).start()

    def step(tau, carry):
        e = tau - r

        @pl.when(jnp.logical_and(e >= 0, e < items))
        def _():
            target = n - 1 - e // q_count
            pass_on(e, r, target, target, forward, recv_p, send_p)

        f = tau - rr

        @pl.when(jnp.logical_and(f >= 0, f < items))
        def _():
            target = n - 1 - f // q_count
            pass_on(f, rr, target, n - 1 - target, backward, recv_s, send_s)

        return carry

    lax.fori_loop(0, items + n - 1, step, 0)

    def drain(e, carry):
        target = n - 1 - e // q_count

        @pl.when(r < target)
        def _():
            forward(e).wait_send()

        @pl.when(rr < target)
        def _():
            backward(e).wait_send()

        return carry

    out_ref[...] = (own[r] * (1.0 / root)).astype(BF16)
    lax.fori_loop(0, items, drain, 0)


def second_factor(n, root, a, pe):
    rank = a.shape[1]
    width = pe.shape[1]
    q_count = max(1, 16 // n)
    items = ((n - 1) * q_count, rank // n, width // q_count)
    vm = pl.BlockSpec(memory_space=pltpu.VMEM)
    dma = pltpu.SemaphoreType.DMA
    return pl.pallas_call(
        functools.partial(second_kernel, n, q_count, root),
        out_shape=jax.ShapeDtypeStruct((rank // n, width), BF16),
        in_specs=[vm, vm],
        out_specs=vm,
        scratch_shapes=[pltpu.VMEM((n, rank // n, width), F32)]
        + [pltpu.VMEM(items, BF16)] * 4
        + [dma((items[0],))] * 4,
        compiler_params=pltpu.CompilerParams(collective_id=1, has_side_effects=True, vmem_limit_bytes=48 << 20),
        name="second_factor",
    )(a, pe)


def shards(n, nc, weight, update, keep_codes, chol_factor, sketch):
    root = math.sqrt(weight.shape[0] * n)
    pe, sample, gram = sample_and_gram(n, nc, weight, update, keep_codes, chol_factor, sketch)
    adapter_a = finish(gram, sample, root)
    return (adapter_a, second_factor(n, root, adapter_a, pe))


def solution(mesh):
    in_specs = (
        P(("layers", "rows"), "cols"),
        P(("layers", "rows"), "cols"),
        P(("layers", "rows"), "cols"),
        P(("layers", "cols"), "rows"),
        P("rows", None),
    )
    out_specs = (P(("layers", "rows"), None), P(("layers", "rows"), "cols"))
    body = functools.partial(shards, mesh.shape["rows"], mesh.shape["cols"])
    return jax.shard_map(body, mesh=mesh, in_specs=in_specs, out_specs=out_specs, check_vma=False)
```

time: 394 us -> 158 us (0.40)
  waiting for transfers between devices: 249 us -> 0 us
  Pallas kernels: 0 us -> 153 us
  other arithmetic: 69.9 us -> 0 us
  matrix products: 34.3 us -> 0 us
  local copies, waits for them, and re-layouts: 24.2 us -> 4.32 us
  between operations: 15.1 us -> 0.66 us
    reduce_scatter x2 -> x0, waiting for transfers between devices: 155 us -> none  [the longest x1 79.6 us: shards(): lax.psum_scatter(jnp.dot(chol_factor, sketch, preferred_element_type=jnp....]
    pallas_call x0 -> x3, Pallas kernels: none -> 153 us  [the longest x1 85.3 us: sample_and_gram(): pl.pallas_call(functools.partial(sample_kernel, n, nc), out_shape=(jax.Sh...]
    psum x2 -> x0, waiting for transfers between devices: 66.3 us -> none  [the longest x1 35.5 us: shards(): gram_matrix = lax.psum(gram_of(sample), 'rows')]
    another operation x10 -> x0, other arithmetic: 57.6 us -> none  [the longest x6 34.6 us: finish(): lower_factor = jnp.linalg.cholesky(gram_matrix)]
    dot_general x4 -> x0, matrix products: 29.7 us -> none  [the longest x1 17 us: shards(): jnp.dot(chol_factor, sketch, preferred_element_type=jnp.float32)]
    all_gather x1 -> x0, waiting for transfers between devices: 27 us -> none  [shards(): whitened = lax.all_gather(own_share, 'rows', axis=0, tiled=True)]
    another operation x10 -> x0, local copies, waits for them, and re-layouts: 11.2 us -> none
    unnamed x8 -> x0, other arithmetic: 7.12 us -> none
  transfers between devices with their start and end apart: 5 -> 0, of which waited for: 5 -> 0; matrix products, arithmetic and copies ran while one was open for 5% -> 0% of each run, Pallas kernels for 0% -> 0%
where the time goes in v1:
time: 158 us
  Pallas kernels  153 us (97%)
  local copies, waits for them, and re-layouts  4.32 us (3%)
    pallas_call x1, Pallas kernels, sample_and_gram(): pl.pallas_call(functools.partial(sample_kernel, n, nc), out_shape=(jax.Sh...  85.3 us
    pallas_call x1, Pallas kernels, second_factor(): pl.pallas_call(functools.partial(second_kernel, n, q_count, root), out_sh...  45.2 us
    pallas_call x1, Pallas kernels, finish(): pl.pallas_call(functools.partial(finish_kernel, root), out_shape=jax.Shap...  22.2 us
    unnamed x7, local copies, waits for them, and re-layouts  4.32 us

profile of v1, /device:TPU:0, one launch (start us, length us, event | category | flops | bytes accessed | tf_op | source)
XLA Modules:
  0.0 157.8 jit_solution(14786288713058090858)
XLA Ops:
  0.6 0.0 copy-start.1
  0.6 1.0 copy-done.1
  1.7 85.3 %sample_and_gram.1 = (bf16[256,4096]{1,0:T(8,128)(2,1)}, f32[256,256]{1,0:T(8,128)S(1)}, f32[256,256]{1,0:T(8,128)S(1)}) custom-call(bf16[256,4096]{1,0:T(8,128)(2,1)} %w_hbm.1, bf16[256,4096]{1,0:T(8,128)(2,1)} %u_hbm.1, s32[256,512]{1,0:T(8,128)S(1)} %copy-done.1, bf16[4096,4096]{1,0:T(8,128)(2,1)} %l_hbm.1, bf16[4096,256]{1,0:T(8,128)(2,1)} %s_hbm.1), custom_call_target="tpu_custom_call" | custom-call | tf_op jit(solution)/shard_map/sample_and_gram/pallas_call | solution.py:293
  87.0 22.2 %shard_map.68.a_ref = bf16[256,256]{1,0:T(8,128)(2,1)} custom-call(f32[256,256]{1,0:T(8,128)S(1)} %get-tuple-element.5.g_ref, f32[256,256]{1,0:T(8,128)S(1)} %get-tuple-element.6.s_ref), custom_call_target="tpu_custom_call" | custom-call | tf_op jit(solution)/shard_map/pallas_call | solution.py:78
  109.3 0.0 copy-start
  109.3 1.6 %copy-done = bf16[256,4096]{1,0:T(8,128)(2,1)S(1)} copy-done((bf16[256,4096]{1,0:T(8,128)(2,1)S(1)}, bf16[256,4096]{1,0:T(8,128)(2,1)}, u32[]{:S(2)}) %copy-start) | copy-done | bytes 2097176
  110.9 0.0 copy-start.2
  110.9 0.9 copy-done.2
  111.8 45.2 %second_factor.1 = bf16[64,4096]{1,0:T(8,128)(2,1)S(1)} custom-call(bf16[256,256]{1,0:T(8,128)(2,1)S(1)} %copy-done.2, bf16[256,4096]{1,0:T(8,128)(2,1)S(1)} %copy-done), custom_call_target="tpu_custom_call" | custom-call | tf_op jit(solution)/shard_map/second_factor/pallas_call | solution.py:419
  157.0 0.8 copy.8
Async XLA Ops:
  0.6 1.0 copy-start.1
  109.3 1.6 %copy-start = (bf16[256,4096]{1,0:T(8,128)(2,1)S(1)}, bf16[256,4096]{1,0:T(8,128)(2,1)}, u32[]{:S(2)}) copy-start(bf16[256,4096]{1,0:T(8,128)(2,1)} %get-tuple-element.7.pe_ref) | copy-start | bytes 6291460
  110.9 0.9 copy-start.2

commit v2 on v1

--- a/solution.py
+++ b/solution.py
@@ -11,7 +11,10 @@
 MESH = pl.DeviceIdType.MESH
 F32 = jnp.float32
 BF16 = jnp.bfloat16
-NCHUNK = 8
+NCHUNK = 32
+SUBS = 4
+LAG = 3
+GATHER = 3
 WORDS = 128
 
 HI = lax.Precision.HIGHEST
@@ -66,23 +69,6 @@
 
         lax.fori_loop(0, seg // 8, body, 0)
 
-def finish_kernel(root, g_ref, s_ref, a_ref, m_ref, w_ref):
-    n = g_ref.shape[0]
-    m_ref[...] = g_ref[...]
-    chol_steps(m_ref, w_ref, n, 4)
-    basis = lax.dot_general(s_ref[...], w_ref[...], (((1,), (1,)), ((), ())), precision=HI, preferred_element_type=jnp.float32)
-    a_ref[...] = (root * basis).astype(jnp.bfloat16)
-
-def finish(gram, sample, root):
-    n = gram.shape[0]
-    return pl.pallas_call(functools.partial(finish_kernel, root),
-        out_shape=jax.ShapeDtypeStruct(sample.shape, jnp.bfloat16),
-        in_specs=[pl.BlockSpec(memory_space=pltpu.VMEM)] * 2,
-        out_specs=pl.BlockSpec(memory_space=pltpu.VMEM),
-        scratch_shapes=[pltpu.VMEM((n, n), jnp.float32)] * 2,
-        compiler_params=pltpu.CompilerParams(vmem_limit_bytes=32 << 20))(gram, sample)
-
-
 def copy_to(src, dst, send, recv, axis, index):
     return pltpu.make_async_remote_copy(
         src_ref=src, dst_ref=dst, send_sem=send, recv_sem=recv, device_id={axis: index}, device_id_type=MESH
@@ -100,10 +86,12 @@
     pl.semaphore_wait(barrier, count)
 
 
-def sample_kernel(
-    n, nc, w_hbm, u_hbm, k_hbm, l_hbm, s_hbm, pe_ref, sample_ref, gram_ref,
+def whole_kernel(
+    n, nc, q_count, gq, root, w_hbm, u_hbm, k_hbm, l_hbm, s_hbm, a_ref, out_ref, pe_ref,
     w_v, u_v, k_v, s_v, l_v, expand, own, recv_p, recv_s, send_p, send_s, acc, rs_recv, samp, gpart, gz, gfull,
     in_sem, l_sem, sp_sem, rp_sem, ss_sem, rsv_sem, a_send, a_recv, b_send, b_recv, c_send, c_recv, d_send, d_recv,
+    m_ref, inv_ref, a_l, a_r, pe_l, pe_r, own2, own_l, own_r, q_recv_p, q_recv_s, q_send_p, q_send_s,
+    qsp_sem, qrp_sem, qss_sem, qrs_sem, n_send, n_recv,
 ):
     r = lax.axis_index("rows")
     c = lax.axis_index("cols")
@@ -118,8 +106,10 @@
     give_s = jnp.logical_and(r > 0, nonzero)
     rr = n - 1 - r
 
+    big = SUBS * ck
+
     def load(t):
-        return pltpu.make_async_copy(l_hbm.at[pl.ds(pl.multiple_of(t * ck, ck), ck), :], l_v.at[lax.rem(t, 2)], l_sem.at[lax.rem(t, 2)])
+        return pltpu.make_async_copy(l_hbm.at[pl.ds(pl.multiple_of(t * big, big), big), :], l_v.at[lax.rem(t, 2)], l_sem.at[lax.rem(t, 2)])
 
     ins = [pltpu.make_async_copy(a, b, in_sem.at[i]) for i, (a, b) in enumerate(((s_hbm, s_v), (w_hbm, w_v), (u_hbm, u_v), (k_hbm, k_v)))]
     ins[0].start()
@@ -144,21 +134,28 @@
     def backward(j):
         return copy_to(send_s.at[j], recv_s.at[j], ss_sem.at[j], rsv_sem.at[j], "rows", lax.rem(r + n - 1, n))
 
+    def whiten(t):
+        at = pl.ds(pl.multiple_of(t * SUBS, SUBS), SUBS)
+
+        @pl.when(nonzero)
+        def _():
+            @pl.when((t + 1) * SUBS < NCHUNK)
+            def _():
+                load(t + 1).start()
+
+            load(t).wait()
+            own[at] = jnp.dot(l_v[lax.rem(t, 2)], s_v[...], preferred_element_type=F32).reshape(SUBS, ck, rank)
+
+        @pl.when(jnp.logical_not(nonzero))
+        def _():
+            own[at] = jnp.zeros((SUBS, ck, rank), F32)
+
     def step(t, carry):
-        @pl.when(jnp.logical_and(t < NCHUNK, nonzero))
-        def _():
-            @pl.when(t + 1 < NCHUNK)
-            def _():
-                load(t + 1).start()
-
-            load(t).wait()
-            own[t] = jnp.dot(l_v[lax.rem(t, 2)], s_v[...], preferred_element_type=F32)
-
-        @pl.when(jnp.logical_and(t < NCHUNK, jnp.logical_not(nonzero)))
-        def _():
-            own[t] = jnp.zeros((ck, rank), F32)
-
-        p = t - r
+        @pl.when(jnp.logical_and(t % SUBS == 0, t < NCHUNK))
+        def _():
+            whiten(t // SUBS)
+
+        p = t - LAG * r
 
         @pl.when(jnp.logical_and(p >= 0, p < NCHUNK))
         def _():
@@ -178,7 +175,7 @@
 
                 forward(p).start()
 
-        s = t - rr
+        s = t - LAG * rr
 
         @pl.when(jnp.logical_and(s >= 0, s < NCHUNK))
         def _():
@@ -198,9 +195,10 @@
 
                 backward(s).start()
 
-        @pl.when(t < pe_steps)
-        def _():
-            codes = k_v[:, pl.ds(pl.multiple_of(t * WORDS, WORDS), WORDS)]
+        @pl.when(jnp.logical_and(t % SUBS == 1, t < pe_steps * SUBS))
+        def _():
+            i = t // SUBS
+            codes = k_v[:, pl.ds(pl.multiple_of(i * WORDS, WORDS), WORDS)]
             second = lax.shift_right_logical(codes * 43, 8)
             first = codes - 6 * second
             table = jnp.full(codes.shape, 0xCA6953, jnp.int32)
@@ -209,12 +207,12 @@
             packed = (low + 16 * high).astype(F32).astype(BF16)
             spread = jnp.dot(packed, expand[...], preferred_element_type=F32).astype(jnp.int32)
             bit = jnp.left_shift(1, lax.broadcasted_iota(jnp.int32, spread.shape, 1) & 7)
-            at = pl.ds(pl.multiple_of(t * 8 * WORDS, 8 * WORDS), 8 * WORDS)
+            at = pl.ds(pl.multiple_of(i * 8 * WORDS, 8 * WORDS), 8 * WORDS)
             wv = w_v[:, at].astype(F32)
             uv = u_v[:, at].astype(F32)
             pe_ref[:, at] = (wv - jnp.where((spread & bit) != 0, wv + uv, 0.0)).astype(BF16)
 
-        m = t - jnp.maximum(r, rr)
+        m = t - LAG * jnp.maximum(r, rr)
 
         @pl.when(jnp.logical_and(m >= 0, m < NCHUNK))
         def _():
@@ -226,12 +224,16 @@
             def _():
                 own[m] = own[m] + recv_s[m].astype(F32)
 
-            part = jnp.dot(pe_ref[:, pl.ds(pl.multiple_of(m * ck, ck), ck)], own[m].astype(BF16), preferred_element_type=F32)
-            acc[...] += part.reshape(acc.shape)
+            @pl.when(m % SUBS == SUBS - 1)
+            def _():
+                i = m // SUBS
+                whole = own[pl.ds(pl.multiple_of(i * SUBS, SUBS), SUBS)].reshape(big, rank).astype(BF16)
+                part = jnp.dot(pe_ref[:, pl.ds(pl.multiple_of(i * big, big), big)], whole, preferred_element_type=F32)
+                acc[...] += part.reshape(acc.shape)
 
         return carry
 
-    lax.fori_loop(0, NCHUNK + n - 1, step, 0)
+    lax.fori_loop(0, NCHUNK + LAG * (n - 1), step, 0)
 
     def drain(j, carry):
         @pl.when(r < n - 1)
@@ -266,7 +268,6 @@
     samp[c] = total
     sent += exchange(lambda p: samp.at[c], samp, b_send, b_recv, "cols", nc, c)
     sample = samp[...].reshape(local_rows, rank)
-    sample_ref[...] = sample
     gpart[...] = lax.dot_general(
         sample, sample, (((0,), (0,)), ((), ())), precision=HI, preferred_element_type=F32
     ).reshape(gpart.shape)
@@ -276,35 +277,187 @@
         total = total + gz[p]
     gfull[c] = total
     sent += exchange(lambda p: gfull.at[c], gfull, d_send, d_recv, "cols", nc, c)
-    gram_ref[...] = gfull[...].reshape(rank, rank)
+    share, cq = out_ref.shape[0], width // q_count
+    gw = gq * cq
+    nq = q_count - gq
+    plain = (n - 1) * nq
+    lo, hi = lax.rem(r + n - 1, n), lax.rem(r + 1, n)
+    near = [
+        copy_to(pe_ref.at[:, 0:gw], pe_l, n_send.at[0], n_recv.at[0], "rows", hi),
+        copy_to(pe_ref.at[:, 0:gw], pe_r, n_send.at[1], n_recv.at[1], "rows", lo),
+        copy_to(a_ref, a_l, n_send.at[2], n_recv.at[2], "rows", hi),
+        copy_to(a_ref, a_r, n_send.at[3], n_recv.at[3], "rows", lo),
+    ]
+
+    def start_near(i):
+        @pl.when(r < n - 1)
+        def _():
+            near[i].start()
+
+        @pl.when(r > 0)
+        def _():
+            near[i + 1].start()
+
+    start_near(0)
+    m_ref[...] = gfull[...].reshape(rank, rank)
+    chol_steps(m_ref, inv_ref, rank, 4)
+    basis = lax.dot_general(sample, inv_ref[...], (((1,), (1,)), ((), ())), precision=HI, preferred_element_type=F32)
+    a_ref[...] = (root * basis).astype(BF16)
+    start_near(2)
+
+    def times(a, pe, at):
+        return lax.dot_general(a[...], pe[:, at], (((0,), (0,)), ((), ())), preferred_element_type=F32).reshape(n, share, cq)
+
+    def column(q):
+        return pl.ds(pl.multiple_of(q * cq, cq), cq)
+
+    def fill(i, carry):
+        at = column(q_count - 1 - i)
+        own2[:, :, at] = times(a_ref, pe_ref, at)
+        return carry
+
+    lax.fori_loop(0, q_count, fill, 0)
+
+    def q_forward(b):
+        return copy_to(q_send_p.at[b], q_recv_p.at[b], qsp_sem.at[b], qrp_sem.at[b], "rows", hi)
+
+    def q_backward(b):
+        return copy_to(q_send_s.at[b], q_recv_s.at[b], qss_sem.at[b], qrs_sem.at[b], "rows", lo)
+
+    def first_sends(e, carry):
+        at = column(gq + e % nq)
+
+        @pl.when(r == 0)
+        def _():
+            q_send_p[e] = own2[n - 1 - e // nq, :, at].astype(BF16)
+            q_forward(e).start()
+
+        @pl.when(rr == 0)
+        def _():
+            q_send_s[e] = own2[e // nq, :, at].astype(BF16)
+            q_backward(e).start()
+
+        return carry
+
+    lax.fori_loop(0, plain, first_sends, 0)
+
+    def pass_on(b, first, least, place, target, t, base, at, copy, recv, send):
+        @pl.when(jnp.logical_and(place > first, place <= target))
+        def _():
+            copy(b).wait_recv()
+            base[t, :, at] = base[t, :, at] + recv[b].astype(F32)
+
+        @pl.when(jnp.logical_and(place >= least, place < target))
+        def _():
+            send[b] = base[t, :, at].astype(BF16)
+            copy(b).start()
+
+    def chain(count, per, q0, b0, first, least, base_p, base_s):
+        def step2(tau, carry):
+            e = tau - LAG * r
+
+            @pl.when(jnp.logical_and(e >= 0, e < count))
+            def _():
+                target = n - 1 - e // per
+                pass_on(b0 + e, first, least, r, target, target, base_p, column(q0 + e % per), q_forward, q_recv_p, q_send_p)
+
+            f = tau - LAG * rr
+
+            @pl.when(jnp.logical_and(f >= 0, f < count))
+            def _():
+                target = n - 1 - f // per
+                pass_on(b0 + f, first, least, rr, target, n - 1 - target, base_s, column(q0 + f % per), q_backward, q_recv_s, q_send_s)
+
+            return carry
+
+        lax.fori_loop(0, count + LAG * (n - 1), step2, 0)
+
+    @pl.when(r > 0)
+    def _():
+        near[0].wait_recv()
+        near[2].wait_recv()
+        for q in range(gq):
+            own_l[:, :, q * cq:(q + 1) * cq] = times(a_l, pe_l, slice(q * cq, (q + 1) * cq))
+
+    @pl.when(r < n - 1)
+    def _():
+        near[1].wait_recv()
+        near[3].wait_recv()
+        for q in range(gq):
+            own_r[:, :, q * cq:(q + 1) * cq] = times(a_r, pe_r, slice(q * cq, (q + 1) * cq))
+
+    chain((n - 1) * gq, gq, 0, plain, 1, 1, own_l, own_r)
+    chain(plain, nq, gq, 0, 0, 1, own2, own2)
+
+    @pl.when(r > 0)
+    def _():
+        own2[r, :, 0:gw] = own2[r, :, 0:gw] + own_l[r]
+
+    @pl.when(r < n - 1)
+    def _():
+        own2[r, :, 0:gw] = own2[r, :, 0:gw] + own_r[r]
+
+    out_ref[...] = (own2[r] * (1.0 / root)).astype(BF16)
+
     lax.fori_loop(0, NCHUNK, drain, 0)
+
+    def drain_second(count, per, b0, first):
+        def one_drain(e, carry):
+            target = n - 1 - e // per
+
+            @pl.when(jnp.logical_and(r >= first, r < target))
+            def _():
+                q_forward(b0 + e).wait_send()
+
+            @pl.when(jnp.logical_and(rr >= first, rr < target))
+            def _():
+                q_backward(b0 + e).wait_send()
+
+            return carry
+
+        lax.fori_loop(0, count, one_drain, 0)
+
+    drain_second(plain, nq, 0, 0)
+    drain_second((n - 1) * gq, gq, plain, 1)
+
+    @pl.when(r < n - 1)
+    def _():
+        near[0].wait_send()
+        near[2].wait_send()
+
+    @pl.when(r > 0)
+    def _():
+        near[1].wait_send()
+        near[3].wait_send()
+
     for one in sent:
         one.wait_send()
 
 
-def sample_and_gram(n, nc, weight, update, codes, factor, sketch):
+def adapters(n, nc, root, weight, update, codes, factor, sketch):
     rows, width = weight.shape
     block, depth = factor.shape
     rank = sketch.shape[1]
     ck = block // NCHUNK
     chunks = (NCHUNK, ck, rank)
+    q_count = max(2, 32 // n)
+    gq = max(1, q_count * GATHER // 8)
+    gw = gq * (width // q_count)
+    items = ((n - 1) * q_count, rank // n, width // q_count)
     vm = pl.BlockSpec(memory_space=pltpu.VMEM)
     dma = pltpu.SemaphoreType.DMA
     return pl.pallas_call(
-        functools.partial(sample_kernel, n, nc),
-        out_shape=(
-            jax.ShapeDtypeStruct((rows, width), BF16),
-            jax.ShapeDtypeStruct((rows, rank), F32),
-            jax.ShapeDtypeStruct((rank, rank), F32),
-        ),
+        functools.partial(whole_kernel, n, nc, q_count, gq, root),
+        out_shape=(jax.ShapeDtypeStruct((rows, rank), BF16), jax.ShapeDtypeStruct((rank // n, width), BF16)),
         in_specs=[pl.BlockSpec(memory_space=pl.ANY)] * 5,
-        out_specs=(vm, vm, vm),
+        out_specs=(vm, vm),
         scratch_shapes=[
+            pltpu.VMEM((rows, width), BF16),
             pltpu.VMEM((rows, width), BF16),
             pltpu.VMEM((rows, width), BF16),
             pltpu.VMEM(codes.shape, jnp.int32),
             pltpu.VMEM(sketch.shape, BF16),
-            pltpu.VMEM((2, ck, depth), BF16),
+            pltpu.VMEM((2, SUBS * ck, depth), BF16),
             pltpu.VMEM((WORDS, 8 * WORDS), BF16),
             pltpu.VMEM(chunks, F32),
             pltpu.VMEM(chunks, BF16),
@@ -331,109 +484,27 @@
             dma((n,)),
             dma((nc,)),
             dma((nc,)),
-        ],
-        compiler_params=pltpu.CompilerParams(collective_id=0, has_side_effects=True, vmem_limit_bytes=52 << 20),
-        name="sample_and_gram",
+            pltpu.VMEM((rank, rank), F32),
+            pltpu.VMEM((rank, rank), F32),
+            pltpu.VMEM((rows, rank), BF16),
+            pltpu.VMEM((rows, rank), BF16),
+            pltpu.VMEM((rows, gw), BF16),
+            pltpu.VMEM((rows, gw), BF16),
+            pltpu.VMEM((n, rank // n, width), F32),
+            pltpu.VMEM((n, rank // n, gw), F32),
+            pltpu.VMEM((n, rank // n, gw), F32),
+        ]
+        + [pltpu.VMEM(items, BF16)] * 4
+        + [dma((items[0],))] * 4
+        + [dma((4,))] * 2,
+        compiler_params=pltpu.CompilerParams(collective_id=0, has_side_effects=True, vmem_limit_bytes=58 << 20),
+        name="adapters",
     )(weight, update, codes, factor, sketch)
-
-
-def second_kernel(n, q_count, root, a_ref, pe_ref, out_ref, own, recv_p, recv_s, send_p, send_s, sp_sem, rp_sem, ss_sem, rs_sem):
-    r = lax.axis_index("rows")
-    rr = n - 1 - r
-    share, width = out_ref.shape
-    cq = width // q_count
-    items = (n - 1) * q_count
-    a_t = a_ref[...]
-
-    def fill(q, carry):
-        at = pl.ds(pl.multiple_of(q * cq, cq), cq)
-        part = lax.dot_general(a_t, pe_ref[:, at], (((0,), (0,)), ((), ())), preferred_element_type=F32)
-        own[:, :, at] = part.reshape(n, share, cq)
-        return carry
-
-    lax.fori_loop(0, q_count, fill, 0)
-    greet((("rows", n),))
-
-    def forward(e):
-        return copy_to(send_p.at[e], recv_p.at[e], sp_sem.at[e], rp_sem.at[e], "rows", lax.rem(r + 1, n))
-
-    def backward(e):
-        return copy_to(send_s.at[e], recv_s.at[e], ss_sem.at[e], rs_sem.at[e], "rows", lax.rem(r + n - 1, n))
-
-    def pass_on(e, place, target, t, copy, recv, send):
-        at = pl.ds(pl.multiple_of((e % q_count) * cq, cq), cq)
-
-        @pl.when(jnp.logical_and(place > 0, place <= target))
-        def _():
-            copy(e).wait_recv()
-            own[t, :, at] = own[t, :, at] + recv[e].astype(F32)
-
-        @pl.when(place < target)
-        def _():
-            send[e] = own[t, :, at].astype(BF16)
-            copy(e).start()
-
-    def step(tau, carry):
-        e = tau - r
-
-        @pl.when(jnp.logical_and(e >= 0, e < items))
-        def _():
-            target = n - 1 - e // q_count
-            pass_on(e, r, target, target, forward, recv_p, send_p)
-
-        f = tau - rr
-
-        @pl.when(jnp.logical_and(f >= 0, f < items))
-        def _():
-            target = n - 1 - f // q_count
-            pass_on(f, rr, target, n - 1 - target, backward, recv_s, send_s)
-
-        return carry
-
-    lax.fori_loop(0, items + n - 1, step, 0)
-
-    def drain(e, carry):
-        target = n - 1 - e // q_count
-
-        @pl.when(r < target)
-        def _():
-            forward(e).wait_send()
-
-        @pl.when(rr < target)
-        def _():
-            backward(e).wait_send()
-
-        return carry
-
-    out_ref[...] = (own[r] * (1.0 / root)).astype(BF16)
-    lax.fori_loop(0, items, drain, 0)
-
-
-def second_factor(n, root, a, pe):
-    rank = a.shape[1]
-    width = pe.shape[1]
-    q_count = max(1, 16 // n)
-    items = ((n - 1) * q_count, rank // n, width // q_count)
-    vm = pl.BlockSpec(memory_space=pltpu.VMEM)
-    dma = pltpu.SemaphoreType.DMA
-    return pl.pallas_call(
-        functools.partial(second_kernel, n, q_count, root),
-        out_shape=jax.ShapeDtypeStruct((rank // n, width), BF16),
-        in_specs=[vm, vm],
-        out_specs=vm,
-        scratch_shapes=[pltpu.VMEM((n, rank // n, width), F32)]
-        + [pltpu.VMEM(items, BF16)] * 4
-        + [dma((items[0],))] * 4,
-        compiler_params=pltpu.CompilerParams(collective_id=1, has_side_effects=True, vmem_limit_bytes=48 << 20),
-        name="second_factor",
-    )(a, pe)
 
 
 def shards(n, nc, weight, update, keep_codes, chol_factor, sketch):
     root = math.sqrt(weight.shape[0] * n)
-    pe, sample, gram = sample_and_gram(n, nc, weight, update, keep_codes, chol_factor, sketch)
-    adapter_a = finish(gram, sample, root)
-    return (adapter_a, second_factor(n, root, adapter_a, pe))
+    return adapters(n, nc, root, weight, update, keep_codes, chol_factor, sketch)
 
 
 def solution(mesh):

time: 158 us -> 144 us (0.911); the launches traced: 158 us -> 142 us
  Pallas kernels: 153 us -> 138 us
    pallas_call x3 -> x1, Pallas kernels: 153 us -> 138 us  [adapters(): pl.pallas_call(functools.partial(whole_kernel, n, nc, q_count, gq, root),...]
    unnamed x7 -> x2, local copies, waits for them, and re-layouts: 4.32 us -> 3.44 us
where the time goes in v2:
time: 144 us; the launch traced here: 142 us
  Pallas kernels  138 us (96%)
  local copies, waits for them, and re-layouts  3.44 us (2%)
    pallas_call x1, Pallas kernels, adapters(): pl.pallas_call(functools.partial(whole_kernel, n, nc, q_count, gq, root),...  138 us
    unnamed x2, local copies, waits for them, and re-layouts  3.44 us

profile of v2, /device:TPU:0, one launch (start us, length us, event | category | flops | bytes accessed | tf_op | source)
XLA Modules:
  0.0 142.1 jit_solution(17686825192580710768)
XLA Ops:
  0.6 138.0 %adapters.1 = (bf16[256,256]{1,0:T(8,128)(2,1)}, bf16[64,4096]{1,0:T(8,128)(2,1)}) custom-call(bf16[256,4096]{1,0:T(8,128)(2,1)} %w_hbm.1, bf16[256,4096]{1,0:T(8,128)(2,1)} %u_hbm.1, s32[256,512]{1,0:T(8,128)} %k_hbm.1, bf16[4096,4096]{1,0:T(8,128)(2,1)} %l_hbm.1, bf16[4096,256]{1,0:T(8,128)(2,1)} %s_hbm.1), custom_call_target="tpu_custom_call" | custom-call | tf_op jit(solution)/shard_map/adapters/pallas_call | solution.py:449
  138.7 1.6 %copy.9 = bf16[256,256]{1,0:T(8,128)(2,1)} copy(bf16[256,256]{1,0:T(8,128)(2,1)} %get-tuple-element.4) | data formatting | bytes 262144
  140.3 1.9 %copy.10 = bf16[64,4096]{1,0:T(8,128)(2,1)} copy(bf16[64,4096]{1,0:T(8,128)(2,1)} %get-tuple-element.5) | data formatting | bytes 1048576

commit v3 on v2

--- a/solution.py
+++ b/solution.py
@@ -300,7 +300,7 @@
 
     start_near(0)
     m_ref[...] = gfull[...].reshape(rank, rank)
-    chol_steps(m_ref, inv_ref, rank, 4)
+    chol_steps(m_ref, inv_ref, rank, 8)
     basis = lax.dot_general(sample, inv_ref[...], (((1,), (1,)), ((), ())), precision=HI, preferred_element_type=F32)
     a_ref[...] = (root * basis).astype(BF16)
     start_near(2)

time: 144 us -> 141 us (0.979)
  Pallas kernels: 138 us -> 136 us
    pallas_call x1, Pallas kernels: 138 us -> 136 us  [adapters(): pl.pallas_call(functools.partial(whole_kernel, n, nc, q_count, gq, root),...]
where the time goes in v3:
time: 141 us; the launch traced here: 140 us
  Pallas kernels  136 us (96%)
  local copies, waits for them, and re-layouts  3.44 us (2%)
    pallas_call x1, Pallas kernels, adapters(): pl.pallas_call(functools.partial(whole_kernel, n, nc, q_count, gq, root),...  136 us
    unnamed x2, local copies, waits for them, and re-layouts  3.44 us

profile of v3, /device:TPU:0, one launch (start us, length us, event | category | flops | bytes accessed | tf_op | source)
XLA Modules:
  0.0 140.0 jit_solution(5479255526637971322)
XLA Ops:
  0.6 135.9 %adapters.1 = (bf16[256,256]{1,0:T(8,128)(2,1)}, bf16[64,4096]{1,0:T(8,128)(2,1)}) custom-call(bf16[256,4096]{1,0:T(8,128)(2,1)} %w_hbm.1, bf16[256,4096]{1,0:T(8,128)(2,1)} %u_hbm.1, s32[256,512]{1,0:T(8,128)} %k_hbm.1, bf16[4096,4096]{1,0:T(8,128)(2,1)} %l_hbm.1, bf16[4096,256]{1,0:T(8,128)(2,1)} %s_hbm.1), custom_call_target="tpu_custom_call" | custom-call | tf_op jit(solution)/shard_map/adapters/pallas_call | solution.py:449
  136.6 1.6 %copy.9 = bf16[256,256]{1,0:T(8,128)(2,1)} copy(bf16[256,256]{1,0:T(8,128)(2,1)} %get-tuple-element.4) | data formatting | bytes 262144
  138.1 1.9 %copy.10 = bf16[64,4096]{1,0:T(8,128)(2,1)} copy(bf16[64,4096]{1,0:T(8,128)(2,1)} %get-tuple-element.5) | data formatting | bytes 1048576
